TPU v7x, 256 devices: a whole 4x4x8 slice. The times are simulated.
256 devices in a mesh: section: 16 (over x_lo, y, core), dp: 16 (over x_hi, z).
Axes of the slice: x: 4 (x_hi: 2, x_lo: 2; x = x_hi * 2 + x_lo), y: 4, z: 8, core: 2. Of those that a mesh axis runs over, the one named last changes fastest.
Arguments:
- activations: bfloat16 [16, 16, 256, 4096], P('section', 'dp'), may hold values from -6 to 6
- gains: float32 [2, 16, 4096], P(None, 'section'), may hold values from 0.1 to 1.9
- kv_weight: bfloat16 [2, 16, 4096, 1024], P(None, 'section', 'dp'), as said below
- lengths: int32 [16, 16], P('section', 'dp'), may hold values from 64 to 256
Outputs:
- advanced: bfloat16 [16, 16, 256, 4096], P('section', 'dp')
Inputs may be any that keep to these rules, and one draw needn't show every extreme that they name: `kv_weight`: projection weights of order one to eight over square root of 4096.
All inputs are finite; a program needn't handle non-finite values.
Results may differ from a plain program's by a relative error of at most 0.022.
Values may be sent and summed in bfloat16 or wider, within the bound.
A program may use at most 128 MiB of HBM per device.

v0:
```python
import jax
import jax.numpy as jnp
from jax import lax
from jax.sharding import PartitionSpec as P

HEAD_DIM = 128
TICKS = 3


def from_behind(shard, axis, by):
    peers = lax.axis_size(axis)
    return lax.ppermute(shard, axis, [(i, (i + by) % peers) for i in range(peers)])


def normalize(block, gain):
    xf = block.astype(jnp.float32)
    factor = lax.rsqrt(jnp.mean(xf * xf, axis=-1, keepdims=True) + 1e-05)
    return (xf, (xf * factor * gain).astype(jnp.bfloat16))


def finish(xf, normed, keyval, length):
    seq = normed.shape[0]
    width = keyval.shape[1] // 2
    groups = width // HEAD_DIM
    keys = keyval[:, :width].reshape(seq, groups, HEAD_DIM)
    values = keyval[:, width:].reshape(seq, groups, HEAD_DIM)
    query = normed.reshape(seq, groups, -1, HEAD_DIM)
    scores = jnp.einsum(
        "qhgd,khd->hgqk", query, keys, preferred_element_type=jnp.float32
    ) * HEAD_DIM ** (-0.5)
    places = jnp.arange(seq, dtype=jnp.int32)
    allowed = (places[None, :] <= places[:, None]) & (places[None, :] < length)
    scores = jnp.where(allowed, scores, -1e30)
    topmost = jnp.max(scores, axis=-1, keepdims=True)
    expo = jnp.exp(scores - topmost)
    probs = (expo / jnp.sum(expo, axis=-1, keepdims=True)).astype(jnp.bfloat16)
    mixed = jnp.einsum("hgqk,khd->qhgd", probs, values, preferred_element_type=jnp.float32).reshape(
        seq, -1
    )
    return (xf + mixed).astype(jnp.bfloat16)


def per_device(activations, gains, kv_weight, lengths):
    block = activations[0, 0]
    length = lengths[0, 0]
    section = lax.axis_index("section")
    local_rows = kv_weight[:, 0]
    gain_rows = gains[:, 0]
    for tick in range(TICKS):
        repeat = (section < tick).astype(jnp.int32)
        gain = lax.dynamic_index_in_dim(gain_rows, repeat, 0, keepdims=False)
        xf, normed = normalize(block, gain)
        shard_rows = lax.dynamic_index_in_dim(local_rows, repeat, 0, keepdims=False)

        def add_rows(total, piece, start, normed=normed):
            return jnp.dot(normed, piece, preferred_element_type=jnp.float32)

        empty = jnp.zeros((normed.shape[0], shard_rows.shape[1]), jnp.float32)
        keyval = add_rows(empty, lax.all_gather(shard_rows, "dp", axis=0, tiled=True), jnp.int32(0))
        block = finish(xf, normed, keyval.astype(jnp.bfloat16), length)
        block, length = from_behind((block, length), "section", 1)
    return block[None, None]


def solution(mesh):
    return jax.shard_map(
        per_device,
        mesh=mesh,
        in_specs=(
            P("section", "dp", None, None),
            P(None, "section", None),
            P(None, "section", "dp", None),
            P("section", "dp"),
        ),
        out_specs=P("section", "dp", None, None),
        check_vma=False,
    )
```

profile of v0, /device:TPU:2, one launch (start us, length us, event | category | flops | bytes accessed | tf_op | source)
XLA Modules:
  0.0 476.3 jit_solution(14156711579204725986)
XLA Ops:
  6.5 2.8 constant_dynamic-slice_fusion.4
  12.5 2.7 copy.38
  15.4 132.4 %all-gather.7.cloned.1.call-done = bf16[1,1,4096,1024]{3,2,1,0:T(8,128)(2,1)} async-done(((bf16[1,1,256,1024]{3,2,1,0:T(8,128)(2,1)}), bf16[1,1,4096,1024]{3,2,1,0:T(8,128)(2,1)}) %all-gather.7.cloned.1.call-update) | async-done | bytes 8388624 | tf_op jit(solution)/shard_map/all_gather | solution.py:59
  147.8 5.7 %fusion.52 = bf16[256,1024]{1,0:T(8,128)(2,1)S(1)} fusion(bf16[1,1,4096,1024]{3,2,1,0:T(8,128)(2,1)} %all-gather.7.cloned.1.call-done, bf16[1,1,256,4096]{3,2,1,0:T(8,128)(2,1)S(1)} %copy-done, f32[4096]{0:T(1024)S(1)} %bitcast.131, f32[256]{0:T(256)S(1)} %add_rsqrt_fusion.2), kind=kOutput, calls=%fused_computation.68 | convolution fusion | flops 2151940096 | bytes 11027456 | tf_op jit(solution)/shard_map/dot_general | solution.py:56
  153.8 5.2 %fusion.41 = f32[4,256,256,8]{2,1,3,0:T(8,128)S(1)} fusion(f32[256,4,8,128]{3,2,1,0:T(8,128)} %bitcast.118, f32[4,8,128]{2,1,0:T(8,128)S(1)} %bitcast.132, f32[256]{0:T(256)S(1)} %add_rsqrt_fusion.2, bf16[256,4,128,1]{2,1,0,3:T(4,128)(2,1)S(1)} %bitcast.125), kind=kOutput, calls=%fused_computation.59 | convolution fusion | flops 540016640 | bytes 12862464 | tf_op jit(solution)/shard_map/qhgd,khd->hgqk/dot_general | solution.py:28
  159.1 2.4 fusion.82
  161.4 2.7 fusion.35
  164.2 5.6 %copy.9 = f32[256,4096]{1,0:T(8,128)} copy(f32[256,4096]{0,1:T(8,128)} %bitcast.121) | data formatting | bytes 8388608 | tf_op jit(solution)/shard_map/reshape | solution.py:37
  169.8 2.8 fusion.18
  172.7 1.6 collective-permute-start.1
  174.2 26.1 %collective-permute-done.1 = s32[]{:T(128)} collective-permute-done((s32[]{:T(128)}, s32[]{:T(128)}, u32[]{:S(2)}, u32[]{:S(2)}) %collective-permute-start.1) | collective-permute-done | bytes 36 | tf_op jit(solution)/shard_map/ppermute | solution.py:12
  202.3 1.8 copy.39
  204.1 78.9 %all-gather.9.cloned.1.call-done = bf16[1,1,4096,1024]{3,2,1,0:T(8,128)(2,1)} async-done(((bf16[1,1,256,1024]{3,2,1,0:T(8,128)(2,1)}), bf16[1,1,4096,1024]{3,2,1,0:T(8,128)(2,1)}) %all-gather.9.cloned.1.call-update) | async-done | bytes 8388624 | tf_op jit(solution)/shard_map/all_gather | solution.py:59
  283.1 5.7 %fusion.57 = bf16[256,1024]{1,0:T(8,128)(2,1)S(1)} fusion(bf16[1,1,4096,1024]{3,2,1,0:T(8,128)(2,1)} %all-gather.9.cloned.1.call-done, bf16[256,4096]{1,0:T(8,128)(2,1)S(1)} %collective-permute-done, f32[4096]{0:T(1024)S(1)} %bitcast.136, f32[256]{0:T(256)S(1)} %add_rsqrt_fusion.1), kind=kOutput, calls=%fused_computation.69 | convolution fusion | flops 2151940096 | bytes 11027456 | tf_op jit(solution)/shard_map/dot_general | solution.py:56
  289.1 2.9 fusion.46
  292.0 2.4 fusion.83
  294.4 2.8 fusion.36
  297.2 5.7 %copy.14 = f32[256,4096]{1,0:T(8,128)} copy(f32[256,4096]{0,1:T(8,128)} %bitcast.122) | data formatting | bytes 8388608 | tf_op jit(solution)/shard_map/reshape | solution.py:37
  302.8 2.8 fusion.22
  305.7 1.6 collective-permute-start.3
  307.3 26.1 %collective-permute-done.3 = s32[]{:T(128)} collective-permute-done((s32[]{:T(128)}, s32[]{:T(128)}, u32[]{:S(2)}, u32[]{:S(2)}) %collective-permute-start.3) | collective-permute-done | bytes 36 | tf_op jit(solution)/shard_map/ppermute | solution.py:12
  334.6 0.8 fusion.63
  335.4 1.8 copy.40
  337.2 81.1 %all-gather.11.cloned.1.call-done = bf16[1,1,4096,1024]{3,2,1,0:T(8,128)(2,1)} async-done(((bf16[1,1,256,1024]{3,2,1,0:T(8,128)(2,1)}), bf16[1,1,4096,1024]{3,2,1,0:T(8,128)(2,1)}) %all-gather.11.cloned.1.call-update) | async-done | bytes 8388624 | tf_op jit(solution)/shard_map/all_gather | solution.py:59
  418.3 5.7 %fusion.60 = bf16[256,1024]{1,0:T(8,128)(2,1)S(1)} fusion(bf16[1,1,4096,1024]{3,2,1,0:T(8,128)(2,1)} %all-gather.11.cloned.1.call-done, bf16[256,4096]{1,0:T(8,128)(2,1)S(1)} %collective-permute-done.2, f32[4096]{0:T(1024)S(1)} %bitcast.134, f32[256]{0:T(256)S(1)} %add_rsqrt_fusion), kind=kOutput, calls=%fused_computation.70 | convolution fusion | flops 2151940096 | bytes 11027456 | tf_op jit(solution)/shard_map/dot_general | solution.py:56
  424.4 2.9 fusion.44
  427.3 2.4 fusion.84
  429.7 2.7 fusion.37
  432.4 5.6 %copy.19 = f32[256,4096]{1,0:T(8,128)} copy(f32[256,4096]{0,1:T(8,128)} %bitcast.123) | data formatting | bytes 8388608 | tf_op jit(solution)/shard_map/reshape | solution.py:37
  438.0 2.7 fusion.26
  440.9 27.6 %collective-permute-done.4 = bf16[256,4096]{1,0:T(8,128)(2,1)S(1)} collective-permute-done((bf16[256,4096]{1,0:T(8,128)(2,1)S(1)}, bf16[256,4096]{1,0:T(8,128)(2,1)S(1)}, u32[]{:S(2)}, u32[]{:S(2)}) %collective-permute-start.4) | collective-permute-done | bytes 2097184 | tf_op jit(solution)/shard_map/ppermute | solution.py:12
  468.4 1.3 copy.59
  (39 shorter events, 6.7 us)
Async XLA Ops:
  6.5 4.3 copy-start
  6.5 141.3 %all-gather.7.cloned.1.call-start = ((), (), s32[]{:S(2)}) async-start(), calls=%async_computation | async-start | bytes 8912896 | tf_op jit(solution)/shard_map/all_gather | solution.py:59
  9.4 273.7 %all-gather.9.cloned.1.call-start = ((), (), s32[]{:S(2)}) async-start(), calls=%async_computation.1 | async-start | bytes 8912896 | tf_op jit(solution)/shard_map/all_gather | solution.py:59
  10.1 408.2 %all-gather.11.cloned.1.call-start = ((), (), s32[]{:S(2)}) async-start(), calls=%async_computation.2 | async-start | bytes 8912896 | tf_op jit(solution)/shard_map/all_gather | solution.py:59
  12.5 2.8 copy-start.1
  172.6 28.5 %collective-permute-start = (bf16[256,4096]{1,0:T(8,128)(2,1)S(1)}, bf16[256,4096]{1,0:T(8,128)(2,1)S(1)}, u32[]{:S(2)}, u32[]{:S(2)}) collective-permute-start(bf16[256,4096]{1,0:T(8,128)(2,1)S(1)} %fusion.18), channel_id=1, source_target_pairs={{0,16},{16,32},{32,48},{48,64},{64,80},{80,96},{96,112},{112,128},... | collective-permute-start | bytes 6291464 | tf_op jit(solution)/shard_map/ppermute | solution.py:12
  172.7 27.7 %collective-permute-start.1 = (s32[]{:T(128)}, s32[]{:T(128)}, u32[]{:S(2)}, u32[]{:S(2)}) collective-permute-start(s32[]{:T(128)} %bitcast.6), channel_id=1, source_target_pairs={{0,16},{16,32},{32,48},{48,64},{64,80},{80,96},{96,112},{112,128},... | collective-permute-start | bytes 20 | tf_op jit(solution)/shard_map/ppermute | solution.py:12
  305.6 28.5 %collective-permute-start.2 = (bf16[256,4096]{1,0:T(8,128)(2,1)S(1)}, bf16[256,4096]{1,0:T(8,128)(2,1)S(1)}, u32[]{:S(2)}, u32[]{:S(2)}) collective-permute-start(bf16[256,4096]{1,0:T(8,128)(2,1)S(1)} %fusion.22), channel_id=1, source_target_pairs={{0,16},{16,32},{32,48},{48,64},{64,80},{80,96},{96,112},{112,128},... | collective-permute-start | bytes 6291464 | tf_op jit(solution)/shard_map/ppermute | solution.py:12
  305.7 27.7 %collective-permute-start.3 = (s32[]{:T(128)}, s32[]{:T(128)}, u32[]{:S(2)}, u32[]{:S(2)}) collective-permute-start(s32[]{:T(128)} %collective-permute-done.1), channel_id=1, source_target_pairs={{0,16},{16,32},{32,48},{48,64},{64,80},{80,96},{96,112},{112,128},... | collective-permute-start | bytes 20 | tf_op jit(solution)/shard_map/ppermute | solution.py:12
  440.8 27.6 %collective-permute-start.4 = (bf16[256,4096]{1,0:T(8,128)(2,1)S(1)}, bf16[256,4096]{1,0:T(8,128)(2,1)S(1)}, u32[]{:S(2)}, u32[]{:S(2)}) collective-permute-start(bf16[256,4096]{1,0:T(8,128)(2,1)S(1)} %fusion.26), channel_id=1, source_target_pairs={{0,16},{16,32},{32,48},{48,64},{64,80},{80,96},{96,112},{112,128},... | collective-permute-start | bytes 6291464 | tf_op jit(solution)/shard_map/ppermute | solution.py:12
Sparse Core Ops, SparseCore 0:
  9.9 137.8 all-gather.6
  150.4 132.6 all-gather.8
  285.7 132.6 all-gather.10
where the time goes:
time: 477 us; the launch traced here: 476 us
  waiting for transfers between devices  374 us (78%)
  matrix products  36.6 us (8%)
  local copies, waits for them, and re-layouts  28.1 us (6%)
  other arithmetic  20.3 us (4%)
  between operations  14 us (3%)
    all_gather x3, waiting for transfers between devices, per_device(): lax.all_gather(shard_rows, 'dp', axis=0, tiled=True)  293 us
    ppermute x5, waiting for transfers between devices, from_behind(): lax.ppermute(shard, axis, [(i, (i + by) % peers) for i in range(peers)])  79.8 us
    dot_general x3, matrix products, add_rows(): return jnp.dot(normed, piece, preferred_element_type=jnp.float32)  17.2 us
    reshape x3, local copies, waits for them, and re-layouts, finish(): jnp.einsum('hgqk,khd->qhgd', probs, values, preferred_element_type=jnp.fl...  16.9 us
    dot_general x3, matrix products, finish(): jnp.einsum('qhgd,khd->hgqk', query, keys, preferred_element_type=jnp.floa...  11.1 us
  transfers between devices with their start and end apart: 8, of which 6 were waited for; matrix products, arithmetic and copies ran while one was open for 12% of the time, Pallas kernels for 0%

commit v1 on v0

--- a/solution.py
+++ b/solution.py
@@ -5,6 +5,13 @@
 
 HEAD_DIM = 128
 TICKS = 3
+
+
+def gather_over(block, mesh_axis, d):
+    peers = lax.axis_size(mesh_axis)
+    shards = jnp.stack([block for _ in range(peers)])
+    shards = lax.all_to_all(shards, mesh_axis, split_axis=0, concat_axis=0)
+    return jnp.concatenate(shards, axis=d)
 
 
 def from_behind(shard, axis, by):
@@ -56,7 +63,7 @@
             return jnp.dot(normed, piece, preferred_element_type=jnp.float32)
 
         empty = jnp.zeros((normed.shape[0], shard_rows.shape[1]), jnp.float32)
-        keyval = add_rows(empty, lax.all_gather(shard_rows, "dp", axis=0, tiled=True), jnp.int32(0))
+        keyval = add_rows(empty, gather_over(shard_rows, "dp", 0), jnp.int32(0))
         block = finish(xf, normed, keyval.astype(jnp.bfloat16), length)
         block, length = from_behind((block, length), "section", 1)
     return block[None, None]

time: 477 us -> 662 us (1.39); the launches traced: 476 us -> 652 us
  blocking collectives: 0 us -> 196 us
  waiting for transfers between devices: 374 us -> 331 us
  starting transfers between devices: 3.51 us -> 26.1 us
  between operations: 14 us -> 0.96 us
  local copies, waits for them, and re-layouts: 28.1 us -> 39 us
    all_gather x3 -> x0, waiting for transfers between devices: 293 us -> none  [per_device(): lax.all_gather(shard_rows, 'dp', axis=0, tiled=True)]
    all_to_all x0 -> x2, waiting for transfers between devices: none -> 214 us  [gather_over(): shards = lax.all_to_all(shards, mesh_axis, split_axis=0, concat_axis=0)]
    all_to_all x0 -> x1, blocking collectives: none -> 196 us  [gather_over(): shards = lax.all_to_all(shards, mesh_axis, split_axis=0, concat_axis=0)]
    ppermute x5, waiting for transfers between devices: 79.8 us -> 117 us  [from_behind(): lax.ppermute(shard, axis, [(i, (i + by) % peers) for i in range(peers)])]
    all_to_all x0 -> x2, starting transfers between devices: none -> 23.8 us  [gather_over(): shards = lax.all_to_all(shards, mesh_axis, split_axis=0, concat_axis=0)]
    another operation x0 -> x3, local copies, waits for them, and re-layouts: none -> 9.67 us  [gather_over(): shards = jnp.stack([block for _ in range(peers)])]
  transfers between devices with their start and end apart: 8 -> 7, of which waited for: 6 -> 5; matrix products, arithmetic and copies ran while one was open for 12% -> 10% of each run, Pallas kernels for 0% -> 0%
where the time goes in v1:
time: 662 us; the launch traced here: 652 us
  waiting for transfers between devices  331 us (50%)
  blocking collectives  196 us (30%)
  local copies, waits for them, and re-layouts  39 us (6%)
  matrix products  36.6 us (6%)
  starting transfers between devices  26.1 us (4%)
  other arithmetic  22.4 us (3%)
    all_to_all x2, waiting for transfers between devices, gather_over(): shards = lax.all_to_all(shards, mesh_axis, split_axis=0, concat_axis=0)  214 us
    all_to_all x1, blocking collectives, gather_over(): shards = lax.all_to_all(shards, mesh_axis, split_axis=0, concat_axis=0)  196 us
    ppermute x5, waiting for transfers between devices, from_behind(): lax.ppermute(shard, axis, [(i, (i + by) % peers) for i in range(peers)])  117 us
    all_to_all x2, starting transfers between devices, gather_over(): shards = lax.all_to_all(shards, mesh_axis, split_axis=0, concat_axis=0)  23.8 us
    dot_general x3, matrix products, add_rows(): return jnp.dot(normed, piece, preferred_element_type=jnp.float32)  17.2 us
    reshape x3, local copies, waits for them, and re-layouts, finish(): jnp.einsum('hgqk,khd->qhgd', probs, values, preferred_element_type=jnp.fl...  16.9 us
  transfers between devices with their start and end apart: 7, of which 5 were waited for; matrix products, arithmetic and copies ran while one was open for 10% of the time, Pallas kernels for 0%

profile of v1, /device:TPU:2, one launch (start us, length us, event | category | flops | bytes accessed | tf_op | source)
XLA Modules:
  0.0 652.1 jit_solution(11066821373599889095)
XLA Ops:
  0.0 1.9 dynamic-slice_bitcast_fusion.2
  3.0 195.8 %all_to_all.15 = bf16[16,256,1024]{2,1,0:T(8,128)(2,1)} all-to-all(bf16[16,256,1024]{2,1,0:T(8,128)(2,1)S(1)} %stack.6), channel_id=1, replica_groups=mesh['section'=16,'dp'=16] {'dp'}, dimensions={0} | all-to-all | bytes 16777216 | tf_op jit(solution)/shard_map/all_to_all | solution.py:13
  198.7 4.3 stack.7
  203.1 4.9 all-to-all-start.1
  209.1 2.5 convert_bitcast_fusion
  211.6 181.0 %all-to-all-done.1 = bf16[16,256,1024]{2,1,0:T(8,128)(2,1)} async-done(((bf16[16,256,1024]{2,1,0:T(8,128)(2,1)}), bf16[16,256,1024]{2,1,0:T(8,128)(2,1)}, u32[]{:S(2)}, u32[]{:S(2)}) %all-to-all-start.1) | async-done | bytes 8388640 | tf_op jit(solution)/shard_map/all_to_all | solution.py:13
  392.6 4.3 stack.8
  396.9 19.0 %all-to-all-start.2 = ((bf16[16,256,1024]{2,1,0:T(8,128)(2,1)}), bf16[16,256,1024]{2,1,0:T(8,128)(2,1)}, u32[]{:S(2)}, u32[]{:S(2)}) async-start(bf16[16,256,1024]{2,1,0:T(8,128)(2,1)} %stack.8), calls=%async_computation.2 | async-start | bytes 16777216 | tf_op jit(solution)/shard_map/all_to_all | solution.py:13
  415.9 4.9 copy.38
  420.9 5.8 fusion.47
  426.9 5.2 fusion.34
  432.2 2.4 fusion.69
  434.5 2.8 fusion.28
  437.3 5.6 copy.9
  442.9 2.7 fusion.9
  447.4 32.2 %collective-permute-done.1 = s32[]{:T(128)} collective-permute-done((s32[]{:T(128)}, s32[]{:T(128)}, u32[]{:S(2)}, u32[]{:S(2)}) %collective-permute-start.1) | collective-permute-done | bytes 36 | tf_op jit(solution)/shard_map/ppermute | solution.py:19
  481.6 1.8 copy.39
  483.4 5.7 convolution_convert_fusion.1
  489.4 2.9 fusion.41
  492.4 2.4 fusion.70
  494.8 2.7 fusion.29
  497.5 5.6 copy.14
  503.1 2.7 fusion.13
  506.3 57.7 %collective-permute-done.3 = s32[]{:T(128)} collective-permute-done((s32[]{:T(128)}, s32[]{:T(128)}, u32[]{:S(2)}, u32[]{:S(2)}) %collective-permute-start.3) | collective-permute-done | bytes 36 | tf_op jit(solution)/shard_map/ppermute | solution.py:19
  567.7 33.0 %all-to-all-done.2 = bf16[16,256,1024]{2,1,0:T(8,128)(2,1)} async-done(((bf16[16,256,1024]{2,1,0:T(8,128)(2,1)}), bf16[16,256,1024]{2,1,0:T(8,128)(2,1)}, u32[]{:S(2)}, u32[]{:S(2)}) %all-to-all-start.2) | async-done | bytes 8388640 | tf_op jit(solution)/shard_map/all_to_all | solution.py:13
  600.7 5.7 convolution_convert_fusion
  606.7 2.9 fusion.39
  609.6 2.4 fusion.71
  612.0 2.7 fusion.30
  614.7 5.6 copy.19
  620.4 2.7 fusion.17
  623.2 27.6 %collective-permute-done.4 = bf16[256,4096]{1,0:T(8,128)(2,1)S(1)} collective-permute-done((bf16[256,4096]{1,0:T(8,128)(2,1)S(1)}, bf16[256,4096]{1,0:T(8,128)(2,1)S(1)}, u32[]{:S(2)}, u32[]{:S(2)}) %collective-permute-start.4) | collective-permute-done | bytes 2097184 | tf_op jit(solution)/shard_map/ppermute | solution.py:19
  (38 shorter events, 11.7 us)
Async XLA Ops:
  203.0 5.5 copy-start
  203.1 189.6 %all-to-all-start.1 = ((bf16[16,256,1024]{2,1,0:T(8,128)(2,1)}), bf16[16,256,1024]{2,1,0:T(8,128)(2,1)}, u32[]{:S(2)}, u32[]{:S(2)}) async-start(bf16[16,256,1024]{2,1,0:T(8,128)(2,1)} %stack.7), calls=%async_computation.1 | async-start | bytes 16777216 | tf_op jit(solution)/shard_map/all_to_all | solution.py:13
  396.9 203.8 %all-to-all-start.2 = ((bf16[16,256,1024]{2,1,0:T(8,128)(2,1)}), bf16[16,256,1024]{2,1,0:T(8,128)(2,1)}, u32[]{:S(2)}, u32[]{:S(2)}) async-start(bf16[16,256,1024]{2,1,0:T(8,128)(2,1)} %stack.8), calls=%async_computation.2 | async-start | bytes 16777216 | tf_op jit(solution)/shard_map/all_to_all | solution.py:13
  415.9 5.0 copy-start.1
  445.7 34.7 %collective-permute-start = (bf16[256,4096]{1,0:T(8,128)(2,1)S(1)}, bf16[256,4096]{1,0:T(8,128)(2,1)S(1)}, u32[]{:S(2)}, u32[]{:S(2)}) collective-permute-start(bf16[256,4096]{1,0:T(8,128)(2,1)S(1)} %fusion.9), channel_id=1, source_target_pairs={{0,16},{16,32},{32,48},{48,64},{64,80},{80,96},{96,112},{112,128},... | collective-permute-start | bytes 6291464 | tf_op jit(solution)/shard_map/ppermute | solution.py:19
  445.8 33.8 %collective-permute-start.1 = (s32[]{:T(128)}, s32[]{:T(128)}, u32[]{:S(2)}, u32[]{:S(2)}) collective-permute-start(s32[]{:T(128)} %bitcast.8), channel_id=1, source_target_pairs={{0,16},{16,32},{32,48},{48,64},{64,80},{80,96},{96,112},{112,128},... | collective-permute-start | bytes 20 | tf_op jit(solution)/shard_map/ppermute | solution.py:19
  505.8 58.8 %collective-permute-start.2 = (bf16[256,4096]{1,0:T(8,128)(2,1)S(1)}, bf16[256,4096]{1,0:T(8,128)(2,1)S(1)}, u32[]{:S(2)}, u32[]{:S(2)}) collective-permute-start(bf16[256,4096]{1,0:T(8,128)(2,1)S(1)} %fusion.13), channel_id=1, source_target_pairs={{0,16},{16,32},{32,48},{48,64},{64,80},{80,96},{96,112},{112,128},... | collective-permute-start | bytes 6291464 | tf_op jit(solution)/shard_map/ppermute | solution.py:19
  505.9 58.0 %collective-permute-start.3 = (s32[]{:T(128)}, s32[]{:T(128)}, u32[]{:S(2)}, u32[]{:S(2)}) collective-permute-start(s32[]{:T(128)} %collective-permute-done.1), channel_id=1, source_target_pairs={{0,16},{16,32},{32,48},{48,64},{64,80},{80,96},{96,112},{112,128},... | collective-permute-start | bytes 20 | tf_op jit(solution)/shard_map/ppermute | solution.py:19
  623.1 27.6 %collective-permute-start.4 = (bf16[256,4096]{1,0:T(8,128)(2,1)S(1)}, bf16[256,4096]{1,0:T(8,128)(2,1)S(1)}, u32[]{:S(2)}, u32[]{:S(2)}) collective-permute-start(bf16[256,4096]{1,0:T(8,128)(2,1)S(1)} %fusion.17), channel_id=1, source_target_pairs={{0,16},{16,32},{32,48},{48,64},{64,80},{80,96},{96,112},{112,128},... | collective-permute-start | bytes 6291464 | tf_op jit(solution)/shard_map/ppermute | solution.py:19
